TPU v7x, 256 devices: a whole 4x4x8 slice. The times are simulated.
256 devices in a mesh: section: 16 (over z_hi, y, core), dp: 16 (over x, z_lo).
Axes of the slice: x: 4, y: 4, z: 8 (z_hi: 2, z_lo: 4; z = z_hi * 4 + z_lo), core: 2. Of those that a mesh axis runs over, the one named last changes fastest.
Arguments:
- handoff: bfloat16 [16, 4096, 2048], P('section', 'dp'), may hold values from -6 to 6
- memory_slot: bfloat16 [16, 4096, 2048], P('section', 'dp'), may hold values from -6 to 6
- memory_length: int32 [16, 16], P('section', 'dp'), may hold values from 32 to 256
- saved_input: bfloat16 [16, 4096, 2048], P('section', 'dp'), may hold values from -6 to 6
- saved_memory: bfloat16 [16, 4096, 2048], P('section', 'dp'), may hold values from -6 to 6
- saved_length: int32 [16, 16], P('section', 'dp'), may hold values from 32 to 256
- grad_handoff: bfloat16 [16, 4096, 2048], P('section', 'dp'), may hold values from -6 to 6
- memory_grad_partial: float32 [16, 4096, 2048], P('section', 'dp'), may hold values from -6 to 6
- section_weight: bfloat16 [16, 2048, 2048], P('section', 'dp'), may hold values from -40 to 40
- section_gain: float32 [16, 2048], P('section'), may hold values from 0.5 to 1.5
Outputs:
- section_output: bfloat16 [16, 4096, 2048], P('section', 'dp')
- input_grad: bfloat16 [16, 4096, 2048], P('section', 'dp')
- memory_grad: float32 [16, 4096, 2048], P('section', 'dp')
- weight_grad: float32 [16, 2048, 2048], P('section', 'dp')
- gain_grad: float32 [16, 2048], P('section', 'dp')
All inputs are finite; a program needn't handle non-finite values.
Results may differ from a plain program's by a relative error of at most 0.033.
The roundings to bfloat16 on the way count: a program that leaves them out, or rounds other values in their place, can miss the bound.
Values may be sent and summed in bfloat16 or wider, within the bound.
No kernel may reach another device: no remote copies, remote signals or barrier semaphores. Data moves between devices by JAX's collectives and lax.ppermute only.
A program may use at most 192 MiB of HBM per device.

v0:
```python
import jax
import jax.numpy as jnp
from jax import lax
from jax.sharding import PartitionSpec as P

HEADS = 32
HEAD = 64


epsilon = 1e-06


def passed_along(value, axis, steps):
    count = lax.axis_size(axis)
    pairs = [(source, (source + steps) % count) for source in range(count)]
    return lax.ppermute(value, axis, pairs)


def normalize(values):
    values = values.astype(jnp.float32)
    inverse = lax.rsqrt(jnp.mean(values * values, axis=-1, keepdims=True) + epsilon)
    return (values * inverse, inverse)


def attend(queries, keys_bf, values, length):
    count = queries.shape[0]
    query_heads = queries.reshape(count, HEADS, HEAD)
    key_heads = keys_bf.reshape(count, HEADS, HEAD)
    value_heads = values.reshape(count, HEADS, HEAD)
    scores = jnp.einsum(
        "qhd,khd->hqk", query_heads, key_heads, preferred_element_type=jnp.float32
    ) * HEAD ** (-0.5)
    valid = jnp.arange(count, dtype=jnp.int32) < length
    scores = jnp.where(valid[None, None, :], scores, -1e30)
    weights = jax.nn.softmax(scores, axis=-1)
    weights_bf = weights.astype(jnp.bfloat16)
    mixed = jnp.einsum("hqk,khd->qhd", weights_bf, value_heads, preferred_element_type=jnp.float32)
    return (
        mixed.reshape(count, HEADS * HEAD),
        weights,
        weights_bf,
        query_heads,
        key_heads,
        value_heads,
    )


def encode(inputs, weight, gain_vector):
    normed, inverse = normalize(inputs)
    projected = jnp.dot(
        (normed * gain_vector).astype(jnp.bfloat16), weight, preferred_element_type=jnp.float32
    )
    return (inputs.astype(jnp.float32) + jax.nn.gelu(projected)).astype(jnp.bfloat16)


def decode(targets, memory, length, weight, gain_vector):
    normed, inverse = normalize(targets)
    queries = jnp.dot(
        (normed * gain_vector).astype(jnp.bfloat16), weight, preferred_element_type=jnp.float32
    ).astype(jnp.bfloat16)
    key_normed, key_inverse = normalize(memory)
    mixed = attend(queries, key_normed.astype(jnp.bfloat16), memory, length)[0]
    return (targets.astype(jnp.float32) + mixed).astype(jnp.bfloat16)


def norm_back(grad_normed, normed, inverse):
    return inverse * grad_normed - normed * inverse * jnp.mean(
        grad_normed * normed, axis=-1, keepdims=True
    )


def encode_back(inputs, cotangent, weight, gain_vector):
    normed, inverse = normalize(inputs)
    lowered = (normed * gain_vector).astype(jnp.bfloat16)
    projected = jnp.dot(lowered, weight, preferred_element_type=jnp.float32)
    gelu_back = jax.vjp(jax.nn.gelu, projected)[1]
    grad_proj = gelu_back(cotangent)[0].astype(jnp.bfloat16)
    grad_lowered = jnp.dot(grad_proj, weight.T, preferred_element_type=jnp.float32)
    gain_term = jnp.sum(grad_lowered * normed, axis=0)
    grad_inputs = cotangent + norm_back(grad_lowered * gain_vector, normed, inverse)
    return (
        grad_inputs.astype(jnp.bfloat16),
        lowered,
        grad_proj,
        gain_term,
        jnp.zeros_like(cotangent),
    )


def decode_back(targets, memory, length, cotangent, carried, weight, gain_vector):
    count = targets.shape[0]
    normed, inverse = normalize(targets)
    lowered = (normed * gain_vector).astype(jnp.bfloat16)
    queries = jnp.dot(lowered, weight, preferred_element_type=jnp.float32).astype(jnp.bfloat16)
    key_normed, key_inverse = normalize(memory)
    keys_bf = key_normed.astype(jnp.bfloat16)
    mixed, weights, weights_bf, query_heads, key_heads, value_heads = attend(
        queries, keys_bf, memory, length
    )
    grad_heads = cotangent.astype(jnp.bfloat16).reshape(count, HEADS, HEAD)
    grad_weights = jnp.einsum(
        "qhd,khd->hqk", grad_heads, value_heads, preferred_element_type=jnp.float32
    )
    grad_scores = weights * (grad_weights - jnp.sum(grad_weights * weights, axis=-1, keepdims=True))
    grad_scores = (grad_scores * HEAD ** (-0.5)).astype(jnp.bfloat16)
    grad_queries = (
        jnp.einsum("hqk,khd->qhd", grad_scores, key_heads, preferred_element_type=jnp.float32)
        .reshape(count, HEADS * HEAD)
        .astype(jnp.bfloat16)
    )
    grad_keys = jnp.einsum(
        "hqk,qhd->khd", grad_scores, query_heads, preferred_element_type=jnp.float32
    ).reshape(count, HEADS * HEAD)
    grad_values = jnp.einsum(
        "hqk,qhd->khd", weights_bf, grad_heads, preferred_element_type=jnp.float32
    ).reshape(count, HEADS * HEAD)
    memory_term = grad_values + norm_back(grad_keys, key_normed, key_inverse)
    grad_lowered = jnp.dot(grad_queries, weight.T, preferred_element_type=jnp.float32)
    gain_term = jnp.sum(grad_lowered * normed, axis=0)
    grad_inputs = cotangent + norm_back(grad_lowered * gain_vector, normed, inverse)
    return (
        grad_inputs.astype(jnp.bfloat16),
        lowered,
        grad_queries,
        gain_term,
        memory_term + carried,
    )


def on_device(
    handoff,
    memory_slot,
    memory_length,
    saved_input,
    saved_memory,
    saved_length,
    grad_handoff,
    memory_grad_partial,
    section_weight,
    section_gain,
):
    section_index = lax.axis_index("section")
    section_count = lax.axis_size("section")
    encoder_count = section_count // 2
    full_weight = lax.all_gather(section_weight[0], "dp", axis=0, tiled=True)
    gain_vector = section_gain[0]
    incoming, other_slot, lengths = passed_along(
        (handoff[0], memory_slot[0], memory_length[0]), "section", 1
    )

    def forward_run_decoder(unused):
        first_decoder = section_index == encoder_count
        targets = jnp.where(first_decoder, other_slot, incoming)
        memory = jnp.where(first_decoder, incoming, other_slot)
        return decode(targets, memory, lengths[0], full_weight, gain_vector)

    def forward_run_encoder(unused):
        return encode(incoming, full_weight, gain_vector)

    section_result = lax.cond(
        section_index >= encoder_count, forward_run_decoder, forward_run_encoder, 0
    )
    upstream, partial_in = passed_along(
        (grad_handoff[0].astype(jnp.float32), memory_grad_partial[0]), "section", -1
    )

    def backward_run_decoder(unused):
        carried = jnp.where(
            section_index == section_count - 1, jnp.zeros_like(partial_in), partial_in
        )
        return decode_back(
            saved_input[0],
            saved_memory[0],
            saved_length[0, 0],
            upstream,
            carried,
            full_weight,
            gain_vector,
        )

    def backward_run_encoder(unused):
        cotangent = jnp.where(section_index == encoder_count - 1, partial_in, upstream)
        return encode_back(saved_input[0], cotangent, full_weight, gain_vector)

    grad_inputs, lowered, grad_factor, gain_term, memory_term = lax.cond(
        section_index >= encoder_count, backward_run_decoder, backward_run_encoder, 0
    )
    weight_term = jnp.dot(lowered.T, grad_factor, preferred_element_type=jnp.float32)
    weight_sum = lax.psum_scatter(weight_term, "dp", scatter_dimension=0, tiled=True)
    gain_sum = lax.psum_scatter(gain_term, "dp", scatter_dimension=0, tiled=True)
    backward_results = (grad_inputs, memory_term, weight_sum, gain_sum)
    grad_inputs, memory_term, weight_sum, gain_sum = backward_results
    return (
        section_result[None],
        grad_inputs[None],
        memory_term[None],
        weight_sum[None],
        gain_sum[None],
    )


def solution(mesh):
    return jax.shard_map(
        on_device,
        mesh=mesh,
        in_specs=(
            P("section", "dp", None),
            P("section", "dp", None),
            P("section", "dp"),
            P("section", "dp", None),
            P("section", "dp", None),
            P("section", "dp"),
            P("section", "dp", None),
            P("section", "dp", None),
            P("section", "dp", None),
            P("section", None),
        ),
        out_specs=(
            P("section", "dp", None),
            P("section", "dp", None),
            P("section", "dp", None),
            P("section", "dp", None),
            P("section", "dp"),
        ),
        check_vma=False,
    )
```

profile of v0, /device:TPU:25, one launch (start us, length us, event | category | flops | bytes accessed | tf_op | source)
XLA Modules:
  0.0 769.0 jit_solution(18124235925856644536)
XLA Ops:
  7.2 0.7 all-gather.3.cloned.1.call-update
  8.0 3.0 copy.65
  11.6 1.6 bitcast_convert_fusion.1
  13.4 65.7 %collective-permute-done.3 = f32[256,2048]{0,1:T(8,128)} collective-permute-done((f32[256,2048]{0,1:T(8,128)}, f32[256,2048]{0,1:T(8,128)}, u32[]{:S(2)}, u32[]{:S(2)}) %collective-permute-start.3) | collective-permute-done | bytes 2097184 | tf_op jit(solution)/shard_map/ppermute | solution.py:16
  79.1 78.5 %collective-permute-done.4 = f32[256,2048]{1,0:T(8,128)S(1)} collective-permute-done((f32[256,2048]{1,0:T(8,128)}, f32[256,2048]{1,0:T(8,128)S(1)}, u32[]{:S(2)}, u32[]{:S(2)}) %collective-permute-start.4) | collective-permute-done | bytes 2097184 | tf_op jit(solution)/shard_map/ppermute | solution.py:16
  157.6 42.4 %all-gather.3.cloned.1.call-done = bf16[1,2048,2048]{2,1,0:T(8,128)(2,1)} async-done(((bf16[1,128,2048]{2,1,0:T(8,128)(2,1)}), bf16[1,2048,2048]{2,1,0:T(8,128)(2,1)}) %all-gather.3.cloned.1.call-update) | async-done | bytes 8388624 | tf_op jit(solution)/shard_map/all_gather | solution.py:145
  200.1 30.8 %conditional.4 = (bf16[256,2048]{1,0:T(8,128)(2,1)}, f32[2048]{0:T(1024)S(1)}, bf16[1,256,2048]{2,1,0:T(8,128)(2,1)}, f32[1,256,2048]{2,1,0:T(8,128)}, bf16[256,2048]{0,1:T(8,128)(2,1)}) conditional(s32[]{:T(128)} %convert_element_type.104, (bf16[1,256,2048]{2,1,0:T(8,128)(2,1)S(1)}, f32[1,2048]{1,0:T(1,128)S(1)}, s32[]{:T(128)}, ...), branch_computations={%region_7.11_spmd, %region_11.20_spmd} | conditional | flops 5707414528 | bytes 164812448
  200.4 1.3 fusion.42
  201.6 2.9 copy.66
  204.5 8.0 %fusion.55 = bf16[256,2048]{1,0:T(8,128)(2,1)S(1)} fusion(bf16[2048,2048]{1,0:T(8,128)(2,1)} %get-tuple-element.73, bf16[256,2048]{1,0:T(8,128)(2,1)} %fusion.42, f32[256,2048]{1,0:T(8,128)} %copy.66, f32[256,2048]{1,0:T(8,128)S(1)} %get-tuple-element.72, pred[]{:T(512)S(6)} %eq.7), kind=kOutput, calls=%fused_computation.71 | convolution fusion | flops 2158493696 | bytes 14680065 | tf_op jit(solution)/shard_map/cond/branch_0_fun/dot_general | solution.py:75
  212.5 6.5 fusion.48
  219.1 1.8 fusion.56
  220.9 2.3 copy.56
  223.1 1.6 broadcast_in_dim.56.clone
  230.9 9.7 %fusion.118 = f32[2048,2048]{1,0:T(8,128)} fusion(bf16[256,2048]{1,0:T(8,128)(2,1)} %get-tuple-element.94, bf16[256,2048]{0,1:T(8,128)(2,1)} %get-tuple-element.184), kind=kOutput, calls=%fused_computation.146 | convolution fusion | flops 2147483648 | bytes 18874368 | tf_op jit(solution)/shard_map/dot_general | solution.py:188
  240.6 1.2 copy-done.8
  241.8 1.3 copy.62
  243.1 131.1 %collective-permute-start = (bf16[256,2048]{0,1:T(8,128)(2,1)}, bf16[256,2048]{0,1:T(8,128)(2,1)S(1)}, u32[]{:S(2)}, u32[]{:S(2)}) collective-permute-start(bf16[256,2048]{0,1:T(8,128)(2,1)} %bitcast.110), channel_id=1, source_target_pairs={{0,16},{16,32},{32,48},{48,64},{64,80},{80,96},{96,112},{112,128},... | collective-permute-start | bytes 3145736 | tf_op jit(solution)/shard_map/ppermute | solution.py:16
  376.2 49.6 %collective-permute-done = bf16[256,2048]{0,1:T(8,128)(2,1)S(1)} collective-permute-done((bf16[256,2048]{0,1:T(8,128)(2,1)}, bf16[256,2048]{0,1:T(8,128)(2,1)S(1)}, u32[]{:S(2)}, u32[]{:S(2)}) %collective-permute-start) | collective-permute-done | bytes 1048608 | tf_op jit(solution)/shard_map/ppermute | solution.py:16
  425.8 38.8 %collective-permute-done.2 = s32[1]{0:T(128)} collective-permute-done((s32[1]{0:T(128)}, s32[1]{0:T(128)}, u32[]{:S(2)}, u32[]{:S(2)}) %collective-permute-start.2) | collective-permute-done | bytes 36 | tf_op jit(solution)/shard_map/ppermute | solution.py:16
  464.6 8.2 %conditional.3 = (bf16[1,256,2048]{2,1,0:T(8,128)(2,1)}) conditional(s32[]{:T(128)} %convert_element_type.104, (bf16[256,2048]{0,1:T(8,128)(2,1)S(1)}, f32[1,2048]{1,0:T(1,128)S(1)}, bf16[2048,2048]{1,0:T(8,128)(2,1)}) %tuple.85, (s32[]{:T(128)}, bf16[256,2048]{0,1:T(8,128)(2,1)S(1)}, bf16[256,2048]{0,1:T(8,128)(2,1)S(1)}, s32[1]{0:T(128)}, ...), branch_computations={%region_0.0_spmd, %region_2.7_spmd} | conditional | flops 2706899968 | bytes 59851368 | solution.py:160
  465.5 7.3 fusion.15
  472.8 67.4 %all-reduce = f32[2048]{0:T(1024)S(1)} all-reduce(f32[2048]{0:T(1024)S(1)} %get-tuple-element.96), channel_id=4, replica_groups=mesh['section'=16,'dp'=16] {'dp'}, use_global_device_ids=true, to_apply=%region_21.22.clone | all-reduce | flops 2048 | bytes 16384
  540.9 221.0 %reduce-scatter.2.cloned.1.call-done = f32[128,2048]{1,0:T(8,128)} async-done(((f32[2048,2048]{1,0:T(8,128)}), f32[128,2048]{1,0:T(8,128)}) %reduce-scatter.2.cloned.1.call-update) | async-done | bytes 1048592 | tf_op jit(solution)/shard_map/reduce_scatter | solution.py:189
  (32 shorter events, 4.1 us)
Async XLA Ops:
  7.2 192.9 %all-gather.3.cloned.1.call-start = ((), (), s32[]{:S(2)}) async-start(), calls=%async_computation.2 | async-start | bytes 8912896 | tf_op jit(solution)/shard_map/all_gather | solution.py:145
  7.9 3.7 copy-start.7
  7.9 754.0 %reduce-scatter.2.cloned.1.call-start = ((), (), s32[]{:S(2)}) async-start(), calls=%async_computation.1 | async-start | bytes 17825792 | tf_op jit(solution)/shard_map/reduce_scatter | solution.py:189
  10.9 189.1 %copy-start = (bf16[1,256,2048]{2,1,0:T(8,128)(2,1)S(1)}, bf16[1,256,2048]{2,1,0:T(8,128)(2,1)}, u32[]{:S(2)}) copy-start(bf16[1,256,2048]{2,1,0:T(8,128)(2,1)} %param.17) | copy-start | bytes 3145732
  10.9 189.1 %copy-start.12 = (f32[1,2048]{1,0:T(1,128)S(1)}, f32[1,2048]{1,0:T(1,128)}, u32[]{:S(2)}) copy-start(f32[1,2048]{1,0:T(1,128)} %param.23) | copy-start | bytes 24580
  10.9 68.2 %collective-permute-start.3 = (f32[256,2048]{0,1:T(8,128)}, f32[256,2048]{0,1:T(8,128)}, u32[]{:S(2)}, u32[]{:S(2)}) collective-permute-start(f32[256,2048]{0,1:T(8,128)} %bitcast.36), channel_id=1, source_target_pairs={{0,240},{16,0},{32,16},{48,32},{64,48},{80,64},{96,80},{112,96},{1... | collective-permute-start | bytes 6291464 | tf_op jit(solution)/shard_map/ppermute | solution.py:16
  13.2 144.4 %collective-permute-start.4 = (f32[256,2048]{1,0:T(8,128)}, f32[256,2048]{1,0:T(8,128)S(1)}, u32[]{:S(2)}, u32[]{:S(2)}) collective-permute-start(f32[256,2048]{1,0:T(8,128)} %bitcast_convert_fusion.1), channel_id=1, source_target_pairs={{0,240},{16,0},{32,16},{48,32},{64,48},{80,64},{96,80},{112,96},{1... | collective-permute-start | bytes 6291464 | tf_op jit(solution)/shard_map/ppermute | solution.py:16
  212.5 6.6 copy-start.10
  212.5 6.6 copy-start.3
  240.6 1.2 copy-start.8
  241.8 132.4 %copy-start.9 = (bf16[1,256,2048]{2,1,0:T(8,128)(2,1)S(1)}, bf16[1,256,2048]{2,1,0:T(8,128)(2,1)}, u32[]{:S(2)}) copy-start(bf16[1,256,2048]{2,1,0:T(8,128)(2,1)} %param.15) | copy-start | bytes 3145732
  241.8 133.2 %copy-start.13 = (u32[256]{0:T(256)S(1)}, u32[256]{0:T(256)}, u32[]{:S(2)}) copy-start(u32[256]{0:T(256)} %constant.94) | copy-start | bytes 3076
  243.1 182.7 %collective-permute-start = (bf16[256,2048]{0,1:T(8,128)(2,1)}, bf16[256,2048]{0,1:T(8,128)(2,1)S(1)}, u32[]{:S(2)}, u32[]{:S(2)}) collective-permute-start(bf16[256,2048]{0,1:T(8,128)(2,1)} %bitcast.110), channel_id=1, source_target_pairs={{0,16},{16,32},{32,48},{48,64},{64,80},{80,96},{96,112},{112,128},... | collective-permute-start | bytes 3145736 | tf_op jit(solution)/shard_map/ppermute | solution.py:16
  374.8 89.8 %collective-permute-start.1 = (bf16[256,2048]{0,1:T(8,128)(2,1)S(1)}, bf16[256,2048]{0,1:T(8,128)(2,1)S(1)}, u32[]{:S(2)}, u32[]{:S(2)}) collective-permute-start(bf16[256,2048]{0,1:T(8,128)(2,1)S(1)} %bitcast.109), channel_id=1, source_target_pairs={{0,16},{16,32},{32,48},{48,64},{64,80},{80,96},{96,112},{112,128},... | collective-permute-start | bytes 3145736 | tf_op jit(solution)/shard_map/ppermute | solution.py:16
  374.9 89.7 %collective-permute-start.2 = (s32[1]{0:T(128)}, s32[1]{0:T(128)}, u32[]{:S(2)}, u32[]{:S(2)}) collective-permute-start(s32[1]{0:T(128)} %bitcast.35), channel_id=1, source_target_pairs={{0,16},{16,32},{32,48},{48,64},{64,80},{80,96},{96,112},{112,128},... | collective-permute-start | bytes 20 | tf_op jit(solution)/shard_map/ppermute | solution.py:16
Sparse Core Ops, SparseCore 0:
  9.8 190.2 all-gather.2
  240.7 521.1 reduce-scatter.1
where the time goes:
time: 777 us; the launch traced here: 769 us
  waiting for transfers between devices  497 us (64%)
  starting transfers between devices  132 us (17%)
  blocking collectives  67.4 us (9%)
  matrix products  31.5 us (4%)
  between operations  15 us (2%)
  local copies, waits for them, and re-layouts  14.5 us (2%)
    ppermute x5, waiting for transfers between devices, passed_along(): return lax.ppermute(value, axis, pairs)  233 us
    reduce_scatter x1, waiting for transfers between devices, on_device(): lax.psum_scatter(weight_term, 'dp', scatter_dimension=0, tiled=True)  221 us
    ppermute x5, starting transfers between devices, passed_along(): return lax.ppermute(value, axis, pairs)  132 us
    unnamed x1, blocking collectives  67.4 us
    all_gather x1, waiting for transfers between devices, on_device(): full_weight = lax.all_gather(section_weight[0], 'dp', axis=0, tiled=True)  42.4 us
  transfers between devices with their start and end apart: 7, of which 6 were waited for; matrix products, arithmetic and copies ran while one was open for 2% of the time, Pallas kernels for 0%

commit v1 on v0

v1 whole, which is shorter than its diff:
```python
import functools

import jax
import jax.numpy as jnp
from jax import lax
from jax.experimental import pallas as pl
from jax.experimental.pallas import tpu as pltpu
from jax.sharding import PartitionSpec as P

HEADS = 32
HEAD = 64
D = 2048
ROWS = 256
BF = jnp.bfloat16
F32 = jnp.float32
WIDTH = 512
CHUNKS = D // WIDTH
QUAD = 512

epsilon = 1e-06
GELU_A = 0.7978845608028654
GELU_B = 0.044715

NT = (((1,), (1,)), ((), ()))


def dot(a, b):
    return jnp.dot(a, b, preferred_element_type=F32)


def dot_nt(a, b):
    return lax.dot_general(a, b, NT, preferred_element_type=F32)


def rows_loop(count, step, body):
    def run(index, carry):
        body(pl.ds(pl.multiple_of(index * step, step), step))
        return carry

    lax.fori_loop(0, count // step, run, 0)


def norm_rows(values):
    values = values.astype(F32)
    inverse = lax.rsqrt(jnp.mean(values * values, axis=-1, keepdims=True) + epsilon)
    return values * inverse, inverse


def prologue_back(info, x_ref, m_ref, g_ref, u_ref, ut_ref, k_ref):
    def body(rows):
        normed, _ = norm_rows(x_ref[rows, :])
        u_ref[rows, :] = (normed * g_ref[...]).astype(BF)

    rows_loop(ROWS, 32, body)

    @pl.when(info[0] == 1)
    def _():
        def keys(rows):
            k_ref[rows, :] = norm_rows(m_ref[rows, :])[0].astype(BF)

        rows_loop(ROWS, 32, keys)

    for index in range(D // 256):
        cols = slice(index * 256, index * 256 + 256)
        ut_ref[cols, :] = u_ref[:, cols].T


def prologue_forward(info, h_ref, s_ref, g_ref, u_ref, k_ref):
    first = info[1] == 1

    def body(rows):
        y = jnp.where(first, s_ref[rows, :].astype(F32), h_ref[rows, :].astype(F32))
        u_ref[rows, :] = (norm_rows(y)[0] * g_ref[...]).astype(BF)

    rows_loop(ROWS, 32, body)

    @pl.when(info[0] == 1)
    def _():
        def keys(rows):
            m = jnp.where(first, h_ref[rows, :].astype(F32), s_ref[rows, :].astype(F32))
            k_ref[rows, :] = norm_rows(m)[0].astype(BF)

        rows_loop(ROWS, 32, keys)


def project(info, base, u_ref, s_ref, r_ref, z_ref):
    width = s_ref.shape[1]
    for tile in range(width // 256):
        cols = slice(tile * 256, tile * 256 + 256)
        total = None
        for index in range(4):
            part = s_ref if index < 2 else r_ref
            first = QUAD * (index % 2)
            place = pl.multiple_of(info[base + index] * QUAD, QUAD)
            term = dot(u_ref[:, pl.ds(place, QUAD)], part[first : first + QUAD, cols])
            total = term if total is None else total + term
        z_ref[:, cols] = total


def lane_masks():
    lane = lax.broadcasted_iota(jnp.int32, (ROWS, 128), 1)
    return lane < HEAD, lane >= HEAD


def softmax_parts(scores, length):
    column = lax.broadcasted_iota(jnp.int32, scores.shape, 1)
    scores = jnp.where(column < length, scores, -1e30)
    top = jnp.max(scores, axis=-1, keepdims=True)
    raised = jnp.exp(scores - top)
    return raised * (1.0 / jnp.sum(raised, axis=-1, keepdims=True))


def back_chunk(info, u_ref, ut_ref, s_ref, r_ref, c_ref, k_ref, v_ref, dz_ref, ds_ref, dr_ref, dk_ref, dv_ref, z_ref, *, base):
    project(info, base, u_ref, s_ref, r_ref, z_ref)

    @pl.when(info[0] == 0)
    def _():
        def body(rows):
            z = z_ref[rows, :]
            square = z * z
            t = jnp.tanh(GELU_A * (z + GELU_B * (square * z)))
            slope = 0.5 * (1.0 + t) + (0.5 * GELU_A) * z * (1.0 - t * t) * (1.0 + (3 * GELU_B) * square)
            dz_ref[rows, :] = (c_ref[rows, :].astype(F32) * slope).astype(BF)

        rows_loop(ROWS, 32, body)

    @pl.when(info[0] == 1)
    def _():
        length = info[2]

        def pair(index, carry):
            cols = pl.ds(pl.multiple_of(index * 128, 128), 128)
            q = z_ref[:, cols].astype(BF)
            k = k_ref[:, cols]
            v = v_ref[:, cols]
            do = c_ref[:, cols]
            qt = q.T
            dot_t = do.T
            q_small = (q.astype(F32) * 0.125).astype(BF)
            do_small = (do.astype(F32) * 0.125).astype(BF)
            zero = jnp.zeros((), BF)
            total = None
            dks, dvs = [], []
            for head, mask in enumerate(lane_masks()):
                p = softmax_parts(dot_nt(jnp.where(mask, q_small, zero), k), length)
                dp = dot_nt(jnp.where(mask, do_small, zero), v)
                shift = jnp.sum(dp * p, axis=-1, keepdims=True)
                ds = (p * (dp - shift)).astype(BF)
                pb = p.astype(BF)
                term = dot(ds, jnp.where(mask, k, zero))
                total = term if total is None else total + term
                rows = slice(head * HEAD, head * HEAD + HEAD)
                dks.append(dot(qt[rows, :], ds))
                dvs.append(dot(dot_t[rows, :], pb))
            dz_ref[:, cols] = total.astype(BF)
            dk_ref[:, cols] = jnp.concatenate(dks, axis=0).T
            dv_ref[:, cols] = jnp.concatenate(dvs, axis=0).T
            return carry

        lax.fori_loop(0, WIDTH // 128, pair, 0)

    for index in range(4):
        out = ds_ref if index < 2 else dr_ref
        first = QUAD * (index % 2)
        place = pl.multiple_of(info[base + index] * QUAD, QUAD)
        for tile in range(WIDTH // 256):
            cols = slice(tile * 256, tile * 256 + 256)
            out[first : first + QUAD, cols] = dot(ut_ref[pl.ds(place, QUAD), :], dz_ref[:, cols]).astype(BF)


def forward_chunk(info, u_ref, s_ref, r_ref, h_ref, m_ref, k_ref, old_ref, out_ref, z_ref, *, base):
    project(info, base, u_ref, s_ref, r_ref, z_ref)

    @pl.when(info[0] == 0)
    def _():
        def body(rows):
            z = z_ref[rows, :]
            t = jnp.tanh(GELU_A * (z + GELU_B * (z * z * z)))
            out_ref[rows, :] = (h_ref[rows, :].astype(F32) + 0.5 * z * (1.0 + t)).astype(BF)

        rows_loop(ROWS, 32, body)

    @pl.when(info[0] == 1)
    def _():
        length = info[3]
        first = info[1] == 1

        def pair(index, carry):
            cols = pl.ds(pl.multiple_of(index * 128, 128), 128)
            q = (z_ref[:, cols].astype(BF).astype(F32) * 0.125).astype(BF)
            k = k_ref[:, cols]
            h = h_ref[:, cols].astype(F32)
            m = m_ref[:, cols].astype(F32)
            y = jnp.where(first, m, h)
            v = jnp.where(first, h, m).astype(BF)
            zero = jnp.zeros((), BF)
            total = y
            for mask in lane_masks():
                p = softmax_parts(dot_nt(jnp.where(mask, q, zero), k), length)
                total = total + dot(p.astype(BF), jnp.where(mask, v, zero))
            out_ref[:, cols] = total.astype(BF)
            return carry

        lax.fori_loop(0, WIDTH // 128, pair, 0)


def epilogue(info, *refs):
    dzs, refs = refs[:CHUNKS], refs[CHUNKS:]
    parts, refs = refs[: 2 * CHUNKS], refs[2 * CHUNKS :]
    dks, refs = refs[:CHUNKS], refs[CHUNKS:]
    dvs, refs = refs[:CHUNKS], refs[CHUNKS:]
    x_ref, c_ref, m_ref, a_ref, g_ref, dx_ref, dg_ref, dm_ref, du_ref = refs
    for chunk in range(CHUNKS):
        base = 4 + 4 * (chunk % 2)
        for index in range(4):
            part = parts[2 * chunk + index // 2]
            first = QUAD * (index % 2)
            place = pl.multiple_of(info[base + index] * QUAD, QUAD)
            cols = pl.ds(place, QUAD)
            term = dot_nt(dzs[chunk][...], part[first : first + QUAD, :])
            if chunk == 0:
                du_ref[:, cols] = term
            else:
                du_ref[:, cols] += term
    dg_ref[...] = jnp.zeros_like(dg_ref)

    def body(rows):
        normed, inverse = norm_rows(x_ref[rows, :])
        du = du_ref[rows, :]
        dg_ref[...] += jnp.sum(du * normed, axis=0, keepdims=True)
        h = du * g_ref[...]
        mean = jnp.mean(h * normed, axis=-1, keepdims=True)
        dx_ref[rows, :] = (c_ref[rows, :].astype(F32) + inverse * h - normed * (inverse * mean)).astype(BF)

    rows_loop(ROWS, 32, body)

    @pl.when(info[0] == 0)
    def _():
        dm_ref[...] = jnp.zeros_like(dm_ref)

    @pl.when(info[0] == 1)
    def _():
        def back(rows):
            normed, inverse = norm_rows(m_ref[rows, :])
            dk = jnp.concatenate([ref[rows, :] for ref in dks], axis=1)
            dv = jnp.concatenate([ref[rows, :] for ref in dvs], axis=1)
            mean = jnp.mean(dk * normed, axis=-1, keepdims=True)
            dm_ref[rows, :] = dv + inverse * dk - normed * (inverse * mean) + a_ref[rows, :].astype(F32)

        rows_loop(ROWS, 32, back)


def call(body, info, ins, outs, scratch=(), aliases=None, flops=0, limit=48, name=None):
    def spec(shape, block):
        if block == -1:
            return pl.BlockSpec(memory_space=pl.ANY)
        if block is None:
            return pl.BlockSpec(shape, lambda step, info: (0,) * len(shape))
        return pl.BlockSpec((shape[0], WIDTH), lambda step, info: (0, block))

    size = sum(2 * a.size for a, b in ins if b != -1)
    return pl.pallas_call(
        body,
        grid_spec=pltpu.PrefetchScalarGridSpec(
            num_scalar_prefetch=1,
            grid=(1,),
            in_specs=[spec(a.shape, b) for a, b in ins],
            out_specs=[spec(s, b) for s, _, b in outs],
            scratch_shapes=list(scratch),
        ),
        out_shape=[jax.ShapeDtypeStruct(s, t) for s, t, _ in outs],
        input_output_aliases=aliases or {},
        compiler_params=pltpu.CompilerParams(vmem_limit_bytes=limit * 2**20),
        cost_estimate=pl.CostEstimate(flops=flops, bytes_accessed=size, transcendentals=0),
        name=name,
    )(info, *[a for a, _ in ins])


def dp_permute(value, step):
    pairs = []
    for x in range(4):
        for z in range(4):
            to = step(x, z)
            if to is not None:
                pairs.append((x * 4 + z, to[0] * 4 + to[1]))
    return lax.ppermute(value, "dp", pairs)


def z_swap(x, z):
    return (x, z ^ 1)


def z_middle(x, z):
    return (x, 3 - z) if z in (1, 2) else None


def z_outward(x, z):
    return {1: (x, 0), 2: (x, 3)}.get(z)


def z_inward(x, z):
    return {0: (x, 1), 3: (x, 2)}.get(z)


def x_swap(x, z):
    return (x ^ 1, z)


def x_cross(x, z):
    return (3 - x, z)


def gather_pair(shard, z):
    odd = z % 2 == 1
    high = z >= 2
    outer = (z == 0) | (z == 3)
    other = dp_permute(shard, z_swap)
    pair = jnp.concatenate([jnp.where(odd, other, shard), jnp.where(odd, shard, other)], axis=0)
    inner = dp_permute(pair, z_middle)
    last = dp_permute(inner, z_outward)
    rest = jnp.where(outer, last, inner)
    quad = jnp.concatenate([jnp.where(high, rest, pair), jnp.where(high, pair, rest)], axis=0)
    half = shard.shape[1] // 2
    out = []
    for part, first, second in ((quad[:, :half], x_swap, x_cross), (quad[:, half:], x_cross, x_swap)):
        near = jnp.concatenate([part, dp_permute(part, first)], axis=0)
        out.append((near, dp_permute(near, second)))
    return out


def add(a, b):
    return (a.astype(F32) + b.astype(F32)).astype(BF)


def reduce_pair(terms, z):
    odd = z % 2 == 1
    high = z >= 2
    quads = []
    for (near, far), first, second in ((terms[0], x_cross, x_swap), (terms[1], x_swap, x_cross)):
        came = dp_permute(far, first)
        away = add(near[QUAD:], came[QUAD:])
        back = dp_permute(away, second)
        quads.append((near[:QUAD].astype(F32) + came[:QUAD].astype(F32) + back.astype(F32)).astype(BF))
    quad = jnp.concatenate(quads, axis=1)
    other = jnp.where(high, quad[:256], quad[256:])
    mine = jnp.where(high, quad[256:], quad[:256])
    inward = dp_permute(other, z_inward)
    crossed = dp_permute(add(other, inward), z_middle)
    mine = add(mine, crossed)
    kept = jnp.where(odd, mine[128:], mine[:128])
    given = jnp.where(odd, mine[:128], mine[128:])
    return kept.astype(F32) + dp_permute(given, z_swap).astype(F32)


def on_device(
    handoff,
    memory_slot,
    memory_length,
    saved_input,
    saved_memory,
    saved_length,
    grad_handoff,
    memory_grad_partial,
    section_weight,
    section_gain,
):
    section = lax.axis_index("section")
    replica = lax.axis_index("dp")
    count = lax.axis_size("section")
    half = count // 2
    x, z = replica // 4, replica % 4
    gain = section_gain
    shard = section_weight[0]

    def along(value, pairs):
        return lax.ppermute(value, "section", pairs)

    chunks = []
    for pair in range(CHUNKS // 2):
        chunks += gather_pair(shard[:, pair * 2 * WIDTH : (pair + 1) * 2 * WIDTH], z)

    partial = memory_grad_partial[0].astype(BF)
    upstream = jnp.where(section == half, partial, grad_handoff[0])
    cotangent = along(upstream, [(s, (s - 1) % count) for s in range(count)])
    carried = along(partial, [(s, s - 1) for s in range(half + 1, count)])
    incoming = along(handoff[0], [(s, (s + 1) % count) for s in range(count)])
    slot = along(memory_slot[0], [(s, s + 1) for s in range(half - 1, count - 1)])
    length = along(memory_length[0], [(s, s + 1) for s in range(half - 1, count - 1)])

    swap, cross = x + 1 - 2 * (x % 2), 3 - x
    far = cross + 1 - 2 * (cross % 2)
    is_decoder = (section >= half).astype(jnp.int32)
    is_first = (section == half).astype(jnp.int32)
    head = [is_decoder, is_first, saved_length[0, 0]]
    order = [x, swap, cross, far, x, cross, swap, far]
    zero = jnp.int32(0)
    info_back = jnp.stack([v.astype(jnp.int32) for v in head + [zero] + order])
    info_forward = jnp.stack([v.astype(jnp.int32) for v in head + [length[0]] + order])

    whole = lambda t: ((ROWS, D), t, None)
    u_back, ut_back, k_back = call(
        prologue_back,
        info_back,
        [(saved_input[0], None), (saved_memory[0], None), (gain, None)],
        [whole(BF), ((D, ROWS), BF, None), whole(BF)],
        flops=10**9,
        name="prologue_back",
    )
    back = []
    for index, (near, other) in enumerate(chunks):
        part = ((ROWS, WIDTH), F32, None)
        rows = ((1024, WIDTH), BF, None)
        back.append(
            call(
                functools.partial(back_chunk, base=4 + 4 * (index % 2)),
                info_back,
                [
                    (u_back, None),
                    (ut_back, None),
                    (near, None),
                    (other, None),
                    (cotangent, index),
                    (k_back, index),
                    (saved_memory[0], index),
                ],
                [((ROWS, WIDTH), BF, None), rows, rows, part, part],
                scratch=[pltpu.VMEM((ROWS, WIDTH), F32)],
                flops=8 * 10**9,
                name="back_chunk",
            )
        )
    sums = []
    for pair in range(CHUNKS // 2):
        sums.append(reduce_pair([back[2 * pair + i][1:3] for i in (0, 1)], z))
    weight_sum = jnp.concatenate(sums, axis=1)

    u_forward, k_forward = call(
        prologue_forward,
        info_forward,
        [(incoming, None), (slot, None), (gain, None)],
        [whole(BF), whole(BF)],
        flops=10**9,
        name="prologue_forward",
    )
    result = u_forward
    for index, (near, other) in enumerate(chunks):
        old = [(result, -1)] if index else []
        (result,) = call(
            functools.partial(forward_chunk if index else forward_first, base=4 + 4 * (index % 2)),
            info_forward,
            [(u_forward, None), (near, None), (other, None), (incoming, index), (slot, index), (k_forward, index)] + old,
            [((ROWS, D), BF, index)],
            scratch=[pltpu.VMEM((ROWS, WIDTH), F32)],
            aliases={7: 0} if index else None,
            flops=5 * 10**9,
            name="forward_chunk",
        )

    grad_input, gain_term, memory_term = call(
        epilogue,
        info_back,
        [(b[0], None) for b in back]
        + [(part, None) for both in chunks for part in both]
        + [(b[3], None) for b in back]
        + [(b[4], None) for b in back]
        + [(saved_input[0], None), (cotangent, None), (saved_memory[0], None), (carried, None), (gain, None)],
        [whole(BF), ((1, D), F32, None), whole(F32)],
        scratch=[pltpu.VMEM((ROWS, D), F32)],
        flops=5 * 10**9,
        limit=60,
        name="epilogue",
    )
    gain_sum = lax.psum_scatter(gain_term[0], "dp", scatter_dimension=0, tiled=True)
    return result[None], grad_input[None], memory_term[None], weight_sum[None], gain_sum[None]


def forward_first(info, u_ref, s_ref, r_ref, h_ref, m_ref, k_ref, out_ref, z_ref, *, base):
    forward_chunk(info, u_ref, s_ref, r_ref, h_ref, m_ref, k_ref, None, out_ref, z_ref, base=base)


def solution(mesh):
    rows = P("section", "dp", None)
    one = P("section", "dp")
    return jax.shard_map(
        on_device,
        mesh=mesh,
        in_specs=(rows, rows, one, rows, rows, one, rows, rows, rows, P("section", None)),
        out_specs=(rows, rows, rows, rows, one),
        check_vma=False,
    )
```

time: 777 us -> 340 us (0.44)
  the two profiles are of different devices: /device:TPU:25 before, /device:TPU:128 now
where the time goes in v1:
time: 340 us; the launch traced here: 339 us
  starting transfers between devices  88 us (26%)
  Pallas kernels  86.2 us (25%)
  waiting for transfers between devices  77.3 us (23%)
  blocking collectives  44.7 us (13%)
  other arithmetic  20 us (6%)
  local copies, waits for them, and re-layouts  19.8 us (6%)
    pallas_call x11, Pallas kernels, call(): pl.pallas_call(body, grid_spec=pltpu.PrefetchScalarGridSpec(num_scalar_pr...  86.2 us
    ppermute x28, waiting for transfers between devices, dp_permute(): return lax.ppermute(value, 'dp', pairs)  68.2 us
    ppermute x28, starting transfers between devices, dp_permute(): return lax.ppermute(value, 'dp', pairs)  58.3 us
    unnamed x1, blocking collectives  44.7 us
    ppermute x5, starting transfers between devices, along(): return lax.ppermute(value, 'section', pairs)  29.7 us
    unnamed x105, local copies, waits for them, and re-layouts  17.3 us
    ppermute x5, waiting for transfers between devices, along(): return lax.ppermute(value, 'section', pairs)  9.11 us
  transfers between devices with their start and end apart: 33, of which 12 were waited for; matrix products, arithmetic and copies ran while one was open for 6% of the time, Pallas kernels for 25%

profile of v1, /device:TPU:128, one launch (start us, length us, event | category | flops | bytes accessed | tf_op | source)
XLA Modules:
  0.0 338.5 jit_solution(12703542155369626989)
XLA Ops:
  2.8 7.0 %collective-permute-done.10 = bf16[128,1024]{1,0:T(8,128)(2,1)S(1)} collective-permute-done((bf16[128,1024]{1,0:T(8,128)(2,1)S(1)}, bf16[128,1024]{1,0:T(8,128)(2,1)S(1)}, u32[]{:S(2)}, u32[]{:S(2)}) %collective-permute-start.10) | collective-permute-done | bytes 262176 | tf_op jit(solution)/shard_map/ppermute | solution.py:286
  13.5 4.6 %collective-permute-done.3 = bf16[128,1024]{1,0:T(8,128)(2,1)S(1)} collective-permute-done((bf16[128,1024]{1,0:T(8,128)(2,1)S(1)}, bf16[128,1024]{1,0:T(8,128)(2,1)S(1)}, u32[]{:S(2)}, u32[]{:S(2)}) %collective-permute-start.3) | collective-permute-done | bytes 262176 | tf_op jit(solution)/shard_map/ppermute | solution.py:286
  22.6 3.6 %collective-permute-start.2 = (bf16[256,2048]{1,0:T(8,128)(2,1)}, bf16[256,2048]{1,0:T(8,128)(2,1)}, u32[]{:S(2)}, u32[]{:S(2)}) collective-permute-start(bf16[256,2048]{1,0:T(8,128)(2,1)} %bitcast.9), channel_id=1, source_target_pairs={{112,128},{128,144},{144,160},{160,176},{176,192},{192,208},{208,2... | collective-permute-start | bytes 3145736 | tf_op jit(solution)/shard_map/ppermute | solution.py:376
  27.8 11.1 %collective-permute-done.12 = bf16[256,1024]{1,0:T(8,128)(2,1)S(1)} collective-permute-done((bf16[256,1024]{1,0:T(8,128)(2,1)}, bf16[256,1024]{1,0:T(8,128)(2,1)S(1)}, u32[]{:S(2)}, u32[]{:S(2)}) %collective-permute-start.12) | collective-permute-done | bytes 524320 | tf_op jit(solution)/shard_map/ppermute | solution.py:286
  42.4 22.5 %collective-permute-start.17 = (bf16[256,2048]{1,0:T(8,128)(2,1)}, bf16[256,2048]{1,0:T(8,128)(2,1)}, u32[]{:S(2)}, u32[]{:S(2)}) collective-permute-start(bf16[256,2048]{1,0:T(8,128)(2,1)} %get-tuple-element.61), channel_id=1, source_target_pairs={{0,240},{16,0},{32,16},{48,32},{64,48},{80,64},{96,80},{112,96},{1... | collective-permute-start | bytes 3145736 | tf_op jit(solution)/shard_map/ppermute | solution.py:376
  67.0 9.1 %collective-permute-done = s32[1]{0:T(128)} collective-permute-done((s32[1]{0:T(128)}, s32[1]{0:T(128)}, u32[]{:S(2)}, u32[]{:S(2)}) %collective-permute-start) | collective-permute-done | bytes 36 | tf_op jit(solution)/shard_map/ppermute | solution.py:376
  80.8 11.4 %collective-permute-done.13 = bf16[512,512]{1,0:T(8,128)(2,1)S(1)} collective-permute-done((bf16[512,512]{1,0:T(8,128)(2,1)S(1)}, bf16[512,512]{1,0:T(8,128)(2,1)S(1)}, u32[]{:S(2)}, u32[]{:S(2)}) %collective-permute-start.13) | collective-permute-done | bytes 524320 | tf_op jit(solution)/shard_map/ppermute | solution.py:286
  105.2 4.4 %prologue_forward.1 = (bf16[256,2048]{1,0:T(8,128)(2,1)S(1)}, bf16[256,2048]{1,0:T(8,128)(2,1)S(1)}) custom-call(s32[12]{0:T(128)S(1)} %stack.52.info, bf16[256,2048]{1,0:T(8,128)(2,1)} %collective-permute-done.1.h_ref, bf16[256,2048]{1,0:T(8,128)(2,1)} %collective-permute-done.2.s_ref.m_ref, f32[1,2048]{1,0:T(1,128)S(1)} %copy-done.17), custom_call_target="tpu_custom_call" | custom-call | flops 1000000000 | bytes 2101248 | tf_op jit(solution)/shard_map/prologue_forward/pallas_call | solution.py:262
  113.4 3.8 %collective-permute-done.6 = bf16[512,512]{1,0:T(8,128)(2,1)} collective-permute-done((bf16[512,512]{1,0:T(8,128)(2,1)}, bf16[512,512]{1,0:T(8,128)(2,1)}, u32[]{:S(2)}, u32[]{:S(2)}) %collective-permute-start.6) | collective-permute-done | bytes 524320 | tf_op jit(solution)/shard_map/ppermute | solution.py:286
  120.7 9.8 %back_chunk.4 = (bf16[256,512]{1,0:T(8,128)(2,1)S(1)}, bf16[1024,512]{1,0:T(8,128)(2,1)S(1)}, bf16[1024,512]{1,0:T(8,128)(2,1)}, f32[256,512]{1,0:T(8,128)S(1)}, f32[256,512]{1,0:T(8,128)S(1)}) custom-call(s32[12]{0:T(128)S(1)} %stack.53.info, bf16[256,2048]{1,0:T(8,128)(2,1)S(1)} %copy-done.34, bf16[2048,256]{1,0:T(8,128)(2,1)S(1)} %copy-done.37, ...), custom_call_target="tpu_custom_call" | custom-call | flops 8000000000 | bytes 7340032 | tf_op jit(solution)/shard_map/back_chunk/pallas_call | solution.py:262
  135.0 9.6 %back_chunk.5 = (bf16[256,512]{1,0:T(8,128)(2,1)S(1)}, bf16[1024,512]{1,0:T(8,128)(2,1)S(1)}, bf16[1024,512]{1,0:T(8,128)(2,1)}, f32[256,512]{1,0:T(8,128)S(1)}, f32[256,512]{1,0:T(8,128)S(1)}) custom-call(s32[12]{0:T(128)S(1)} %stack.53.info, bf16[256,2048]{1,0:T(8,128)(2,1)S(1)} %copy-done.34, bf16[2048,256]{1,0:T(8,128)(2,1)S(1)} %copy-done.37, ...), custom_call_target="tpu_custom_call" | custom-call | flops 8000000000 | bytes 7340032 | tf_op jit(solution)/shard_map/back_chunk/pallas_call | solution.py:262
  147.5 7.2 %forward_chunk.4.old_ref = bf16[256,2048]{1,0:T(8,128)(2,1)} custom-call(s32[12]{0:T(128)S(1)} %stack.52.info, bf16[256,2048]{1,0:T(8,128)(2,1)S(1)} %get-tuple-element.33.u_ref, bf16[1024,512]{1,0:T(8,128)(2,1)S(1)} %copy-done.1, bf16[1024,512]{1,0:T(8,128)(2,1)} %collective-permute-done.16.r_ref.refs_5_, bf16[256,2048]{1,0:T(8,128)(2,1)} %collective-permute-done.1.h_ref, ...), custom_call_target="tpu_custom_call" | custom-call | flops 5000000000 | bytes 6291456 | tf_op jit(solution)/shard_map/forward_chunk/pallas_call | solution.py:262
  154.7 6.8 %forward_chunk.5.old_ref = bf16[256,2048]{1,0:T(8,128)(2,1)} custom-call(s32[12]{0:T(128)S(1)} %stack.52.info, bf16[256,2048]{1,0:T(8,128)(2,1)S(1)} %get-tuple-element.33.u_ref, bf16[1024,512]{1,0:T(8,128)(2,1)S(1)} %copy-done.3, bf16[1024,512]{1,0:T(8,128)(2,1)S(1)} %copy-done.12, ...), custom_call_target="tpu_custom_call", output_to_operand_aliasing={{}: (7, {})} | custom-call | flops 5000000000 | bytes 6291456 | tf_op jit(solution)/shard_map/forward_chunk/pallas_call | solution.py:262
  163.7 8.6 %back_chunk.6 = (bf16[256,512]{1,0:T(8,128)(2,1)S(1)}, bf16[1024,512]{1,0:T(8,128)(2,1)S(1)}, bf16[1024,512]{1,0:T(8,128)(2,1)S(1)}, f32[256,512]{1,0:T(8,128)S(1)}, f32[256,512]{1,0:T(8,128)S(1)}) custom-call(s32[12]{0:T(128)S(1)} %stack.53.info, bf16[256,2048]{1,0:T(8,128)(2,1)S(1)} %copy-done.35, bf16[2048,256]{1,0:T(8,128)(2,1)S(1)} %copy-done.38, ...), custom_call_target="tpu_custom_call" | custom-call | flops 8000000000 | bytes 7340032 | tf_op jit(solution)/shard_map/back_chunk/pallas_call | solution.py:262
  177.8 8.6 %back_chunk.7 = (bf16[256,512]{1,0:T(8,128)(2,1)S(1)}, bf16[1024,512]{1,0:T(8,128)(2,1)S(1)}, bf16[1024,512]{1,0:T(8,128)(2,1)S(1)}, f32[256,512]{1,0:T(8,128)S(1)}, f32[256,512]{1,0:T(8,128)S(1)}) custom-call(s32[12]{0:T(128)S(1)} %stack.53.info, bf16[256,2048]{1,0:T(8,128)(2,1)S(1)} %copy-done.35, bf16[2048,256]{1,0:T(8,128)(2,1)S(1)} %copy-done.39, ...), custom_call_target="tpu_custom_call" | custom-call | flops 8000000000 | bytes 7340032 | tf_op jit(solution)/shard_map/back_chunk/pallas_call | solution.py:262
  187.1 7.0 %forward_chunk.6.old_ref = bf16[256,2048]{1,0:T(8,128)(2,1)} custom-call(s32[12]{0:T(128)S(1)} %stack.52.info, bf16[256,2048]{1,0:T(8,128)(2,1)S(1)} %copy-done.31, bf16[1024,512]{1,0:T(8,128)(2,1)S(1)} %copy-done.5, bf16[1024,512]{1,0:T(8,128)(2,1)S(1)} %copy-done.14, ...), custom_call_target="tpu_custom_call", output_to_operand_aliasing={{}: (7, {})} | custom-call | flops 5000000000 | bytes 6291456 | tf_op jit(solution)/shard_map/forward_chunk/pallas_call | solution.py:262
  201.3 11.9 %collective-permute-done.28 = bf16[1024,512]{1,0:T(8,128)(2,1)S(1)} collective-permute-done((bf16[1024,512]{1,0:T(8,128)(2,1)S(1)}, bf16[1024,512]{1,0:T(8,128)(2,1)S(1)}, u32[]{:S(2)}, u32[]{:S(2)}) %collective-permute-start.28) | collective-permute-done | bytes 1048608 | tf_op jit(solution)/shard_map/ppermute | solution.py:286
  214.5 9.9 %collective-permute-done.20 = bf16[512,512]{1,0:T(8,128)(2,1)S(1)} collective-permute-done((bf16[512,512]{1,0:T(8,128)(2,1)S(1)}, bf16[512,512]{1,0:T(8,128)(2,1)S(1)}, u32[]{:S(2)}, u32[]{:S(2)}) %collective-permute-start.20) | collective-permute-done | bytes 524320 | tf_op jit(solution)/shard_map/ppermute | solution.py:286
  227.0 18.7 %collective-permute-start.23 = (bf16[256,1024]{1,0:T(8,128)(2,1)S(1)}, bf16[256,1024]{1,0:T(8,128)(2,1)S(1)}, u32[]{:S(2)}, u32[]{:S(2)}) collective-permute-start(bf16[256,1024]{1,0:T(8,128)(2,1)S(1)} %broadcast_select_fusion.3), channel_id=1, source_target_pairs={{0,1},{3,2},{4,5},{7,6},{8,9},{11,10},{12,13},{15,14},{16,17},{19,... | collective-permute-start | bytes 1572872 | tf_op jit(solution)/shard_map/ppermute | solution.py:286
  247.4 7.7 %collective-permute-start.30 = (bf16[256,1024]{1,0:T(8,128)(2,1)S(1)}, bf16[256,1024]{1,0:T(8,128)(2,1)S(1)}, u32[]{:S(2)}, u32[]{:S(2)}) collective-permute-start(bf16[256,1024]{1,0:T(8,128)(2,1)S(1)} %broadcast_select_fusion.2), channel_id=1, source_target_pairs={{0,1},{3,2},{4,5},{7,6},{8,9},{11,10},{12,13},{15,14},{16,17},{19,... | collective-permute-start | bytes 1572872 | tf_op jit(solution)/shard_map/ppermute | solution.py:286
  255.1 6.8 %forward_chunk.7 = bf16[256,2048]{1,0:T(8,128)(2,1)} custom-call(s32[12]{0:T(128)S(1)} %stack.52.info, bf16[256,2048]{1,0:T(8,128)(2,1)S(1)} %copy-done.31, bf16[1024,512]{1,0:T(8,128)(2,1)S(1)} %copy-done.7, bf16[1024,512]{1,0:T(8,128)(2,1)S(1)} %copy-done.16, bf16[256,2048]{1,0:T(8,128)(2,1)} %collective-permute-done.1.h_ref, ...), custom_call_target="tpu_custom_call", output_to_operand_aliasing={{}: (7, {})} | custom-call | flops 5000000000 | bytes 6291456 | tf_op jit(solution)/shard_map/forward_chunk/pallas_call | solution.py:262
  267.3 14.8 %epilogue.1 = (bf16[256,2048]{1,0:T(8,128)(2,1)}, f32[1,2048]{1,0:T(1,128)}, f32[256,2048]{1,0:T(8,128)}) custom-call(s32[12]{0:T(128)} %copy-done.8, bf16[256,512]{1,0:T(8,128)(2,1)} %copy-done.26, bf16[256,512]{1,0:T(8,128)(2,1)} %copy-done.27, bf16[256,512]{1,0:T(8,128)(2,1)} %copy-done.28, bf16[256,512]{1,0:T(8,128)(2,1)} %copy-done.29, ...), custom_call_target="tpu_custom_call" | custom-call | flops 5000000000 | bytes 15732736 | tf_op jit(solution)/shard_map/epilogue/pallas_call | solution.py:262
  282.1 44.7 %all-reduce = f32[2048]{0:T(1024)S(1)} all-reduce(f32[2048]{0:T(1024)} %bitcast.40), channel_id=2, replica_groups=mesh['section'=16,'dp'=16] {'dp'}, use_global_device_ids=true, to_apply=%region_0.1.clone | all-reduce | flops 2048 | bytes 16384
  331.2 3.4 %collective-permute-done.25 = bf16[128,1024]{1,0:T(8,128)(2,1)S(1)} collective-permute-done((bf16[128,1024]{1,0:T(8,128)(2,1)S(1)}, bf16[128,1024]{1,0:T(8,128)(2,1)S(1)}, u32[]{:S(2)}, u32[]{:S(2)}) %collective-permute-start.25) | collective-permute-done | bytes 262176 | tf_op jit(solution)/shard_map/ppermute | solution.py:286
  (195 shorter events, 83.1 us)
Async XLA Ops:
  22.5 58.3 %collective-permute-start.1 = (bf16[256,2048]{1,0:T(8,128)(2,1)}, bf16[256,2048]{1,0:T(8,128)(2,1)}, u32[]{:S(2)}, u32[]{:S(2)}) collective-permute-start(bf16[256,2048]{1,0:T(8,128)(2,1)} %bitcast.8), channel_id=1, source_target_pairs={{0,16},{16,32},{32,48},{48,64},{64,80},{80,96},{96,112},{112,128},... | collective-permute-start | bytes 3145736 | tf_op jit(solution)/shard_map/ppermute | solution.py:376
  22.6 82.5 %collective-permute-start.2 = (bf16[256,2048]{1,0:T(8,128)(2,1)}, bf16[256,2048]{1,0:T(8,128)(2,1)}, u32[]{:S(2)}, u32[]{:S(2)}) collective-permute-start(bf16[256,2048]{1,0:T(8,128)(2,1)} %bitcast.9), channel_id=1, source_target_pairs={{112,128},{128,144},{144,160},{160,176},{176,192},{192,208},{208,2... | collective-permute-start | bytes 3145736 | tf_op jit(solution)/shard_map/ppermute | solution.py:376
  26.2 52.1 %collective-permute-start.5 = (bf16[256,1024]{1,0:T(8,128)(2,1)}, bf16[256,1024]{1,0:T(8,128)(2,1)S(1)}, u32[]{:S(2)}, u32[]{:S(2)}) collective-permute-start(bf16[256,1024]{1,0:T(8,128)(2,1)} %collective-permute-done.4), channel_id=1, source_target_pairs={{1,0},{2,3},{5,4},{6,7},{9,8},{10,11},{13,12},{14,15},{17,16},{18,... | collective-permute-start | bytes 1572872 | tf_op jit(solution)/shard_map/ppermute | solution.py:286
  39.3 25.7 %collective-permute-start.15 = (bf16[512,512]{1,0:T(8,128)(2,1)S(1)}, bf16[512,512]{1,0:T(8,128)(2,1)S(1)}, u32[]{:S(2)}, u32[]{:S(2)}) collective-permute-start(bf16[512,512]{1,0:T(8,128)(2,1)S(1)} %get-tuple-element.67), channel_id=1, source_target_pairs={{0,4},{1,5},{2,6},{3,7},{4,0},{5,1},{6,2},{7,3},{8,12},{9,13},{10,... | collective-permute-start | bytes 1572872 | tf_op jit(solution)/shard_map/ppermute | solution.py:286
  42.4 78.2 %collective-permute-start.17 = (bf16[256,2048]{1,0:T(8,128)(2,1)}, bf16[256,2048]{1,0:T(8,128)(2,1)}, u32[]{:S(2)}, u32[]{:S(2)}) collective-permute-start(bf16[256,2048]{1,0:T(8,128)(2,1)} %get-tuple-element.61), channel_id=1, source_target_pairs={{0,240},{16,0},{32,16},{48,32},{64,48},{80,64},{96,80},{112,96},{1... | collective-permute-start | bytes 3145736 | tf_op jit(solution)/shard_map/ppermute | solution.py:376
  78.3 42.4 %collective-permute-start.16 = (bf16[1024,512]{1,0:T(8,128)(2,1)S(1)}, bf16[1024,512]{1,0:T(8,128)(2,1)}, u32[]{:S(2)}, u32[]{:S(2)}) collective-permute-start(bf16[1024,512]{1,0:T(8,128)(2,1)S(1)} %pad_maximum_fusion.3.s_ref.refs_4_), channel_id=1, source_target_pairs={{0,12},{1,13},{2,14},{3,15},{4,8},{5,9},{6,10},{7,11},{8,4},{9,5},... | collective-permute-start | bytes 3145736 | tf_op jit(solution)/shard_map/ppermute | solution.py:286
  80.8 29.7 %collective-permute-start.8 = (bf16[512,512]{1,0:T(8,128)(2,1)}, bf16[512,512]{1,0:T(8,128)(2,1)}, u32[]{:S(2)}, u32[]{:S(2)}) collective-permute-start(bf16[512,512]{1,0:T(8,128)(2,1)} %get-tuple-element.69), channel_id=1, source_target_pairs={{0,4},{1,5},{2,6},{3,7},{4,0},{5,1},{6,2},{7,3},{8,12},{9,13},{10,... | collective-permute-start | bytes 1572872 | tf_op jit(solution)/shard_map/ppermute | solution.py:286
  93.1 24.2 %collective-permute-start.6 = (bf16[512,512]{1,0:T(8,128)(2,1)}, bf16[512,512]{1,0:T(8,128)(2,1)}, u32[]{:S(2)}, u32[]{:S(2)}) collective-permute-start(bf16[512,512]{1,0:T(8,128)(2,1)} %get-tuple-element.70), channel_id=1, source_target_pairs={{0,12},{1,13},{2,14},{3,15},{4,8},{5,9},{6,10},{7,11},{8,4},{9,5},... | collective-permute-start | bytes 1572872 | tf_op jit(solution)/shard_map/ppermute | solution.py:286
  105.1 28.9 %collective-permute-start.14 = (bf16[1024,512]{1,0:T(8,128)(2,1)S(1)}, bf16[1024,512]{1,0:T(8,128)(2,1)S(1)}, u32[]{:S(2)}, u32[]{:S(2)}) collective-permute-start(bf16[1024,512]{1,0:T(8,128)(2,1)S(1)} %pad_maximum_fusion.2.s_ref.refs_6_), channel_id=1, source_target_pairs={{0,4},{1,5},{2,6},{3,7},{4,0},{5,1},{6,2},{7,3},{8,12},{9,13},{10,... | collective-permute-start | bytes 3145736 | tf_op jit(solution)/shard_map/ppermute | solution.py:286
  110.5 156.8 %collective-permute-start.18 = (bf16[256,2048]{1,0:T(8,128)(2,1)}, bf16[256,2048]{1,0:T(8,128)(2,1)}, u32[]{:S(2)}, u32[]{:S(2)}) collective-permute-start(bf16[256,2048]{1,0:T(8,128)(2,1)} %get-tuple-element.62), channel_id=1, source_target_pairs={{144,128},{160,144},{176,160},{192,176},{208,192},{224,208},{240,2... | collective-permute-start | bytes 3145736 | tf_op jit(solution)/shard_map/ppermute | solution.py:376
  117.2 44.3 %collective-permute-start.9 = (bf16[1024,512]{1,0:T(8,128)(2,1)S(1)}, bf16[1024,512]{1,0:T(8,128)(2,1)S(1)}, u32[]{:S(2)}, u32[]{:S(2)}) collective-permute-start(bf16[1024,512]{1,0:T(8,128)(2,1)S(1)} %pad_maximum_fusion.1.s_ref.refs_8_), channel_id=1, source_target_pairs={{0,12},{1,13},{2,14},{3,15},{4,8},{5,9},{6,10},{7,11},{8,4},{9,5},... | collective-permute-start | bytes 3145736 | tf_op jit(solution)/shard_map/ppermute | solution.py:286
  120.6 56.2 %collective-permute-start.7 = (bf16[1024,512]{1,0:T(8,128)(2,1)S(1)}, bf16[1024,512]{1,0:T(8,128)(2,1)S(1)}, u32[]{:S(2)}, u32[]{:S(2)}) collective-permute-start(bf16[1024,512]{1,0:T(8,128)(2,1)S(1)} %pad_maximum_fusion.s_ref.refs_10_), channel_id=1, source_target_pairs={{0,4},{1,5},{2,6},{3,7},{4,0},{5,1},{6,2},{7,3},{8,12},{9,13},{10,... | collective-permute-start | bytes 3145736 | tf_op jit(solution)/shard_map/ppermute | solution.py:286
  132.8 61.3 %collective-permute-start.19 = (bf16[1024,512]{1,0:T(8,128)(2,1)}, bf16[1024,512]{1,0:T(8,128)(2,1)S(1)}, u32[]{:S(2)}, u32[]{:S(2)}) collective-permute-start(bf16[1024,512]{1,0:T(8,128)(2,1)} %get-tuple-element.53), channel_id=1, source_target_pairs={{0,12},{1,13},{2,14},{3,15},{4,8},{5,9},{6,10},{7,11},{8,4},{9,5},... | collective-permute-start | bytes 3145736 | tf_op jit(solution)/shard_map/ppermute | solution.py:286
  146.1 50.2 %collective-permute-start.21 = (bf16[1024,512]{1,0:T(8,128)(2,1)}, bf16[1024,512]{1,0:T(8,128)(2,1)}, u32[]{:S(2)}, u32[]{:S(2)}) collective-permute-start(bf16[1024,512]{1,0:T(8,128)(2,1)} %get-tuple-element.55), channel_id=1, source_target_pairs={{0,4},{1,5},{2,6},{3,7},{4,0},{5,1},{6,2},{7,3},{8,12},{9,13},{10,... | collective-permute-start | bytes 3145736 | tf_op jit(solution)/shard_map/ppermute | solution.py:286
  174.7 24.3 %collective-permute-start.26 = (bf16[1024,512]{1,0:T(8,128)(2,1)S(1)}, bf16[1024,512]{1,0:T(8,128)(2,1)}, u32[]{:S(2)}, u32[]{:S(2)}) collective-permute-start(bf16[1024,512]{1,0:T(8,128)(2,1)S(1)} %get-tuple-element.57), channel_id=1, source_target_pairs={{0,12},{1,13},{2,14},{3,15},{4,8},{5,9},{6,10},{7,11},{8,4},{9,5},... | collective-permute-start | bytes 3145736 | tf_op jit(solution)/shard_map/ppermute | solution.py:286
  187.1 26.1 %collective-permute-start.28 = (bf16[1024,512]{1,0:T(8,128)(2,1)S(1)}, bf16[1024,512]{1,0:T(8,128)(2,1)S(1)}, u32[]{:S(2)}, u32[]{:S(2)}) collective-permute-start(bf16[1024,512]{1,0:T(8,128)(2,1)S(1)} %get-tuple-element.59), channel_id=1, source_target_pairs={{0,4},{1,5},{2,6},{3,7},{4,0},{5,1},{6,2},{7,3},{8,12},{9,13},{10,... | collective-permute-start | bytes 3145736 | tf_op jit(solution)/shard_map/ppermute | solution.py:286
  194.3 30.1 %collective-permute-start.20 = (bf16[512,512]{1,0:T(8,128)(2,1)S(1)}, bf16[512,512]{1,0:T(8,128)(2,1)S(1)}, u32[]{:S(2)}, u32[]{:S(2)}) collective-permute-start(bf16[512,512]{1,0:T(8,128)(2,1)S(1)} %add_convert_fusion.11), channel_id=1, source_target_pairs={{0,4},{1,5},{2,6},{3,7},{4,0},{5,1},{6,2},{7,3},{8,12},{9,13},{10,... | collective-permute-start | bytes 1572872 | tf_op jit(solution)/shard_map/ppermute | solution.py:286
  197.5 28.1 %collective-permute-start.22 = (bf16[512,512]{1,0:T(8,128)(2,1)S(1)}, bf16[512,512]{1,0:T(8,128)(2,1)S(1)}, u32[]{:S(2)}, u32[]{:S(2)}) collective-permute-start(bf16[512,512]{1,0:T(8,128)(2,1)S(1)} %add_convert_fusion.9), channel_id=1, source_target_pairs={{0,12},{1,13},{2,14},{3,15},{4,8},{5,9},{6,10},{7,11},{8,4},{9,5},... | collective-permute-start | bytes 1572872 | tf_op jit(solution)/shard_map/ppermute | solution.py:286
  200.1 45.6 %collective-permute-start.27 = (bf16[512,512]{1,0:T(8,128)(2,1)S(1)}, bf16[512,512]{1,0:T(8,128)(2,1)S(1)}, u32[]{:S(2)}, u32[]{:S(2)}) collective-permute-start(bf16[512,512]{1,0:T(8,128)(2,1)S(1)} %add_convert_fusion.5), channel_id=1, source_target_pairs={{0,4},{1,5},{2,6},{3,7},{4,0},{5,1},{6,2},{7,3},{8,12},{9,13},{10,... | collective-permute-start | bytes 1572872 | tf_op jit(solution)/shard_map/ppermute | solution.py:286
  213.3 33.7 %collective-permute-start.29 = (bf16[512,512]{1,0:T(8,128)(2,1)S(1)}, bf16[512,512]{1,0:T(8,128)(2,1)S(1)}, u32[]{:S(2)}, u32[]{:S(2)}) collective-permute-start(bf16[512,512]{1,0:T(8,128)(2,1)S(1)} %add_convert_fusion.3), channel_id=1, source_target_pairs={{0,12},{1,13},{2,14},{3,15},{4,8},{5,9},{6,10},{7,11},{8,4},{9,5},... | collective-permute-start | bytes 1572872 | tf_op jit(solution)/shard_map/ppermute | solution.py:286
  227.0 34.9 %collective-permute-start.23 = (bf16[256,1024]{1,0:T(8,128)(2,1)S(1)}, bf16[256,1024]{1,0:T(8,128)(2,1)S(1)}, u32[]{:S(2)}, u32[]{:S(2)}) collective-permute-start(bf16[256,1024]{1,0:T(8,128)(2,1)S(1)} %broadcast_select_fusion.3), channel_id=1, source_target_pairs={{0,1},{3,2},{4,5},{7,6},{8,9},{11,10},{12,13},{15,14},{16,17},{19,... | collective-permute-start | bytes 1572872 | tf_op jit(solution)/shard_map/ppermute | solution.py:286
  247.4 19.1 %collective-permute-start.30 = (bf16[256,1024]{1,0:T(8,128)(2,1)S(1)}, bf16[256,1024]{1,0:T(8,128)(2,1)S(1)}, u32[]{:S(2)}, u32[]{:S(2)}) collective-permute-start(bf16[256,1024]{1,0:T(8,128)(2,1)S(1)} %broadcast_select_fusion.2), channel_id=1, source_target_pairs={{0,1},{3,2},{4,5},{7,6},{8,9},{11,10},{12,13},{15,14},{16,17},{19,... | collective-permute-start | bytes 1572872 | tf_op jit(solution)/shard_map/ppermute | solution.py:286
  262.9 63.9 %collective-permute-start.24 = (bf16[256,1024]{1,0:T(8,128)(2,1)}, bf16[256,1024]{1,0:T(8,128)(2,1)}, u32[]{:S(2)}, u32[]{:S(2)}) collective-permute-start(bf16[256,1024]{1,0:T(8,128)(2,1)} %add_convert_fusion.7), channel_id=1, source_target_pairs={{1,2},{2,1},{5,6},{6,5},{9,10},{10,9},{13,14},{14,13},{17,18},{18,... | collective-permute-start | bytes 1572872 | tf_op jit(solution)/shard_map/ppermute | solution.py:286
  266.6 61.6 %collective-permute-start.31 = (bf16[256,1024]{1,0:T(8,128)(2,1)S(1)}, bf16[256,1024]{1,0:T(8,128)(2,1)S(1)}, u32[]{:S(2)}, u32[]{:S(2)}) collective-permute-start(bf16[256,1024]{1,0:T(8,128)(2,1)S(1)} %add_convert_fusion.1), channel_id=1, source_target_pairs={{1,2},{2,1},{5,6},{6,5},{9,10},{10,9},{13,14},{14,13},{17,18},{18,... | collective-permute-start | bytes 1572872 | tf_op jit(solution)/shard_map/ppermute | solution.py:286
  (61 other events, 699.0 us)
